TPU v7x, 32 devices: a whole 2x2x4 slice. The times are simulated.
32 devices in a mesh: groups: 1, con: 8 (over z, core), var: 4 (over y, x).
Axes of the slice: x: 2, y: 2, z: 4, core: 2. Of those that a mesh axis runs over, the one named last changes fastest.
Arguments:
- tile_values: bfloat16 [8, 4, 64, 128, 128], P('con', 'var', 'groups'), may hold values from -0.1875 to 0.1875
- tile_row: int32 [8, 4, 64], P('con', 'var', 'groups'), may hold values from 0 to 31
- tile_col: int32 [8, 4, 64], P('con', 'var', 'groups'), may hold values from 0 to 255
- tile_count: int32 [8, 4, 1], P('con', 'var', 'groups'), may hold values from 32 to 64, as said below
- unit_cost: float32 [131072], P(('groups', 'var')), may hold values from -6 to 6
- demand: float32 [8, 32768], P('groups', 'con'), may hold values from -6 to 6
- x_saved: bfloat16 [5, 8, 131072], P(None, 'groups', 'var'), may hold values from 0 to 2
- y_saved: bfloat16 [4, 8, 32768], P(None, 'groups', 'con'), may hold values from 0 to 2
- x_active: int32 [4, 8, 131072], P(None, 'groups', 'var'), may hold values 0 or 1
- y_active: int32 [4, 8, 32768], P(None, 'groups', 'con'), may hold values 0 or 1
- x_cot: float32 [8, 131072], P('groups', 'var'), may hold values from -6 to 6
- y_cot: float32 [8, 32768], P('groups', 'con'), may hold values from -6 to 6
- primal_step: float32 [4], replicated, may hold values from 0.1 to 0.5
- dual_step: float32 [4], replicated, may hold values from 0.1 to 0.5
Outputs:
- x_grad: float32 [8, 131072], P('groups', 'var')
- y_grad: float32 [8, 32768], P('groups', 'con')
- step_grads: float32 [2, 4], P('groups')
Inputs may be any that keep to these rules, and one draw needn't show every extreme that they name: `tile_count`: some device uses all 64 slots. `tile_row`: positions may repeat within a device.
All inputs are finite; a program needn't handle non-finite values. No bound on the sum of `x_active` or of `y_active` on one device may be relied on, other than what follows from the above.
Results may differ from a plain program's by a relative error of at most 0.003.
Values may be sent and summed in bfloat16 or wider, within the bound.
A program may use at most 64 MiB of HBM per device.

v0:
```python
import math

import jax
import jax.numpy as jnp
from jax import lax
from jax.sharding import PartitionSpec as P


def per_device(
    tile_values,
    tile_row,
    tile_col,
    tile_count,
    unit_cost,
    demand,
    x_saved,
    y_saved,
    x_active,
    y_active,
    x_cot,
    y_cot,
    primal_step,
    dual_step,
):
    blocks = tile_values.reshape(tile_values.shape[2:])
    number = blocks.shape[0]
    width = blocks.shape[1]
    row_index = tile_row.reshape(number)
    col_index = tile_col.reshape(number)
    in_use = (jnp.arange(number) < tile_count.reshape(())).astype(jnp.float32)
    rhs_count = x_cot.shape[0]
    row_tiles = demand.shape[1] // width
    col_tiles = x_cot.shape[1] // width
    row_onehot = (row_index[:, None] == jnp.arange(row_tiles)[None, :]).astype(
        jnp.float32
    ) * in_use[:, None]
    col_onehot = (col_index[:, None] == jnp.arange(col_tiles)[None, :]).astype(
        jnp.float32
    ) * in_use[:, None]
    highest = lax.Precision.HIGHEST
    con_count = lax.axis_size("con")
    var_count = lax.axis_size("var")
    scale = 1.0 / math.sqrt(rhs_count * x_cot.shape[1] * var_count)
    y_weight = scale / var_count
    x_weight = scale / con_count
    x_bar = x_cot
    y_bar = y_cot
    collected = []
    for position in reversed(range(primal_step.shape[0])):
        weighted = y_active[position].astype(jnp.float32) * y_bar
        pieces = weighted.astype(jnp.bfloat16).reshape(rhs_count, row_tiles, width)[:, row_index, :]
        product = jnp.einsum("tab,rta->rtb", blocks, pieces, preferred_element_type=jnp.float32)
        summed = jnp.einsum("rtb,tc->rcb", product, col_onehot, precision=highest)
        column_part = lax.psum(summed.reshape(rhs_count, col_tiles * width), "con")
        later = x_saved[position + 1].astype(jnp.float32)
        earlier = x_saved[position].astype(jnp.float32)
        extrapolated = 2.0 * later - earlier
        sigma_term = y_weight * jnp.sum(weighted * demand) - x_weight * jnp.sum(
            column_part * extrapolated
        )
        x_bar = x_bar - 2.0 * dual_step[position] * column_part
        masked = x_active[position].astype(jnp.float32) * x_bar
        apply_pieces = masked.astype(jnp.bfloat16).reshape(rhs_count, col_tiles, width)[
            :, col_index, :
        ]
        apply_product = jnp.einsum(
            "tab,rtb->rta", blocks, apply_pieces, preferred_element_type=jnp.float32
        )
        apply_summed = jnp.einsum("rta,ts->rsa", apply_product, row_onehot, precision=highest)
        row_part = lax.psum(apply_summed.reshape(rhs_count, row_tiles * width), "var")
        tau_term = y_weight * jnp.sum(
            row_part * y_saved[position].astype(jnp.float32)
        ) - x_weight * jnp.sum(masked * unit_cost[None, :])
        y_bar = weighted + primal_step[position] * row_part
        x_bar = masked + dual_step[position] * column_part
        term_pair = jnp.stack([tau_term, sigma_term])
        term_pair = lax.psum(term_pair, ("con", "var"))
        collected.append(term_pair)
    stacked = jnp.stack(collected[::-1], axis=1)
    return (x_bar, y_bar, stacked)


def solution(mesh):
    in_specs = (
        P("con", "var", "groups", None, None),
        P("con", "var", "groups"),
        P("con", "var", "groups"),
        P("con", "var", "groups"),
        P(("groups", "var")),
        P("groups", "con"),
        P(None, "groups", "var"),
        P(None, "groups", "con"),
        P(None, "groups", "var"),
        P(None, "groups", "con"),
        P("groups", "var"),
        P("groups", "con"),
        P(),
        P(),
    )
    out_specs = (P("groups", "var"), P("groups", "con"), P("groups", None))
    return jax.shard_map(
        per_device, mesh=mesh, in_specs=in_specs, out_specs=out_specs, check_vma=False
    )
```

profile of v0, /device:TPU:0, one launch (start us, length us, event | category | flops | bytes accessed | tf_op | source)
XLA Modules:
  0.0 526.0 jit_solution(9981411585800177675)
XLA Ops:
  8.0 0.7 fusion.97
  8.7 1.0 convert_bitcast_fusion.7
  9.7 0.6 gather_fusion
  10.3 0.6 fusion.14
  11.0 1.1 convolution_bitcast_fusion.3
  12.1 1.6 copy.77
  13.7 0.0 all-reduce.12.cloned.1.call-start
  13.8 0.7 fusion.108
  15.1 60.3 %all-reduce.10.cloned.1.call-done = f32[8,32768]{1,0:T(8,128)} async-done(((f32[8,32768]{1,0:T(8,128)}), f32[8,32768]{1,0:T(8,128)}) %all-reduce.10.cloned.1.call-update) | async-done | bytes 1048592 | tf_op jit(solution)/shard_map/psum | solution.py:54
  75.3 2.8 convert_bitcast_fusion.3
  78.2 1.7 gather_fusion.1
  79.9 1.2 fusion.12
  81.1 0.3 convolution_bitcast_fusion.7
  81.4 0.7 copy.81
  82.2 0.0 all-reduce.14.cloned.1.call-start
  82.3 0.6 fusion.107
  82.9 40.4 %all-reduce.12.cloned.1.call-done = f32[8,4096]{1,0:T(8,128)} async-done(((f32[8,4096]{1,0:T(8,128)}), f32[8,4096]{1,0:T(8,128)}) %all-reduce.12.cloned.1.call-update) | async-done | bytes 131088 | tf_op jit(solution)/shard_map/psum | solution.py:70
  123.3 1.6 convert_bitcast_fusion.6
  124.9 0.6 gather_fusion.2
  125.5 0.6 fusion.10
  126.2 1.1 convolution_bitcast_fusion.2
  127.3 1.6 copy.76
  128.9 0.0 all-reduce.16.cloned.1.call-start
  129.6 58.3 %all-reduce.14.cloned.1.call-done = f32[8,32768]{1,0:T(8,128)} async-done(((f32[8,32768]{1,0:T(8,128)}), f32[8,32768]{1,0:T(8,128)}) %all-reduce.14.cloned.1.call-update) | async-done | bytes 1048592 | tf_op jit(solution)/shard_map/psum | solution.py:54
  188.0 3.9 convert_bitcast_fusion.2
  191.9 1.7 gather_fusion.3
  193.5 1.2 fusion.8
  194.7 1.0 convolution_bitcast_fusion.6
  195.7 0.7 copy.80
  196.5 0.0 all-reduce.18.cloned.1.call-start
  196.5 41.0 %all-reduce.16.cloned.1.call-done = f32[8,4096]{1,0:T(8,128)} async-done(((f32[8,4096]{1,0:T(8,128)}), f32[8,4096]{1,0:T(8,128)}) %all-reduce.16.cloned.1.call-update) | async-done | bytes 131088 | tf_op jit(solution)/shard_map/psum | solution.py:70
  237.6 2.2 convert_bitcast_fusion.5
  239.8 1.3 gather_fusion.4
  241.0 1.5 fusion.6
  242.6 1.1 convolution_bitcast_fusion.1
  243.7 1.6 copy.75
  245.3 0.0 all-reduce.20.cloned.1.call-start
  246.0 58.3 %all-reduce.18.cloned.1.call-done = f32[8,32768]{1,0:T(8,128)} async-done(((f32[8,32768]{1,0:T(8,128)}), f32[8,32768]{1,0:T(8,128)}) %all-reduce.18.cloned.1.call-update) | async-done | bytes 1048592 | tf_op jit(solution)/shard_map/psum | solution.py:54
  304.3 4.2 convert_bitcast_fusion.1
  308.5 1.7 gather_fusion.5
  310.2 1.2 fusion.4
  311.4 1.0 convolution_bitcast_fusion.5
  312.4 0.7 copy.79
  313.1 0.2 all-reduce.22.cloned.1.call-start
  313.3 40.9 %all-reduce.20.cloned.1.call-done = f32[8,4096]{1,0:T(8,128)} async-done(((f32[8,4096]{1,0:T(8,128)}), f32[8,4096]{1,0:T(8,128)}) %all-reduce.20.cloned.1.call-update) | async-done | bytes 131088 | tf_op jit(solution)/shard_map/psum | solution.py:70
  354.2 2.5 multiply_reduce_fusion.7
  356.7 1.3 gather_fusion.6
  358.0 1.5 fusion.2
  359.5 1.1 convolution_bitcast_fusion
  360.6 1.6 copy.74
  362.3 0.0 all-reduce.24.cloned.1.call-start
  363.0 58.2 %all-reduce.22.cloned.1.call-done = f32[8,32768]{1,0:T(8,128)} async-done(((f32[8,32768]{1,0:T(8,128)}), f32[8,32768]{1,0:T(8,128)}) %all-reduce.22.cloned.1.call-update) | async-done | bytes 1048592 | tf_op jit(solution)/shard_map/psum | solution.py:54
  421.2 6.5 %fusion.28 = (f32[]{:T(128)}, f32[]{:T(128)}, f32[]{:T(128)}, f32[]{:T(128)}, f32[]{:T(128)}, /*index=5*/f32[]{:T(128)}, f32[]{:T(128)}, f32[]{:T(128)}, f32[8,32768]{1,0:T(8,128)S(1)}) fusion(f32[8,32768]{1,0:T(8,128)} %all-reduce.22.cloned.1.call-done, bf16[5,8,32768]{2,1,0:T(8,128)(2,1)} %param.20, f32[8,32768]{1,0:T(8,128)} %all-reduce.18.cloned.1.call-done, ...), kind=kLoop, calls=%fused_computation.50 | loop fusion | flops 9175032 | bytes 12189736 | tf_op jit(solution)/shard_map/reduce_sum | solution.py:58
  427.7 1.8 convert_bitcast_fusion
  429.5 0.6 gather_fusion.7
  430.1 1.2 fusion
  431.3 0.3 convolution_bitcast_fusion.4
  431.6 0.7 copy.78
  440.0 33.6 %all-reduce.24.cloned.1.call-done = f32[8,4096]{1,0:T(8,128)} async-done(((f32[8,4096]{1,0:T(8,128)}), f32[8,4096]{1,0:T(8,128)}) %all-reduce.24.cloned.1.call-update) | async-done | bytes 131088 | tf_op jit(solution)/shard_map/psum | solution.py:70
  473.5 3.0 fusion.48
  479.0 0.1 maximum_bitcast_fusion
  479.1 0.1 maximum_bitcast_fusion.2
  479.2 39.3 %all-reduce = (f32[2,1]{0,1:T(1,128)S(1)}, f32[2,1]{0,1:T(1,128)S(1)}, f32[2,1]{0,1:T(1,128)S(1)}, f32[2,1]{0,1:T(1,128)S(1)}) all-reduce(f32[2,1]{0,1:T(1,128)S(1)} %get-tuple-element.57, f32[2,1]{0,1:T(1,128)S(1)} %get-tuple-element.56, ...), channel_id=1, replica_groups=mesh['groups'=1,'con'=8,'var'=4] {'con','var'}, use_global_device_ids=true, to_apply=%region_27.0 | all-reduce | flops 8 | bytes 64 | tf_op jit(solution)/shard_map/psum | solution.py:77
  518.5 0.7 copy.17
  (47 shorter events, 0.3 us)
Async XLA Ops:
  7.2 3.2 copy-start
  7.2 3.8 copy-start.11
  7.2 68.1 %all-reduce.10.cloned.1.call-start = ((), (), s32[]{:S(2)}) async-start(), calls=%async_computation | async-start | bytes 2097152 | tf_op jit(solution)/shard_map/psum | solution.py:54
  11.0 2.8 copy-start.14
  11.0 64.3 %copy-start.5 = (f32[8,32768]{1,0:T(8,128)S(1)}, f32[8,32768]{1,0:T(8,128)}, u32[]{:S(2)}) copy-start(f32[8,32768]{1,0:T(8,128)} %param.24) | copy-start | bytes 3145732
  13.7 109.6 %all-reduce.12.cloned.1.call-start = ((), (), s32[]{:S(2)}) async-start(), calls=%async_computation.1 | async-start | bytes 262144 | tf_op jit(solution)/shard_map/psum | solution.py:70
  78.2 2.9 copy-start.12
  78.2 4.1 copy-start.15
  78.2 45.2 %copy-start.3 = (s32[4,8,4096]{2,1,0:T(8,128)S(1)}, s32[4,8,4096]{2,1,0:T(8,128)}, u32[]{:S(2)}) copy-start(s32[4,8,4096]{2,1,0:T(8,128)} %param.23) | copy-start | bytes 1572868
  78.2 45.2 %copy-start.4 = (f32[8,4096]{1,0:T(8,128)S(1)}, f32[8,4096]{1,0:T(8,128)}, u32[]{:S(2)}) copy-start(f32[8,4096]{1,0:T(8,128)} %param.25) | copy-start | bytes 393220
  82.2 105.7 %all-reduce.14.cloned.1.call-start = ((), (), s32[]{:S(2)}) async-start(), calls=%async_computation.2 | async-start | bytes 2097152 | tf_op jit(solution)/shard_map/psum | solution.py:54
  126.2 61.8 %copy-start.1 = (f32[8,32768]{1,0:T(8,128)S(1)}, f32[8,32768]{1,0:T(8,128)}, u32[]{:S(2)}) copy-start(f32[8,32768]{1,0:T(8,128)} %all-reduce.10.cloned.1.call-done) | copy-start | bytes 3145732
  128.9 108.6 %all-reduce.16.cloned.1.call-start = ((), (), s32[]{:S(2)}) async-start(), calls=%async_computation.3 | async-start | bytes 262144 | tf_op jit(solution)/shard_map/psum | solution.py:70
  196.5 107.9 %all-reduce.18.cloned.1.call-start = ((), (), s32[]{:S(2)}) async-start(), calls=%async_computation.4 | async-start | bytes 2097152 | tf_op jit(solution)/shard_map/psum | solution.py:54
  245.3 108.9 %all-reduce.20.cloned.1.call-start = ((), (), s32[]{:S(2)}) async-start(), calls=%async_computation.5 | async-start | bytes 262144 | tf_op jit(solution)/shard_map/psum | solution.py:70
  313.1 108.1 %all-reduce.22.cloned.1.call-start = ((), (), s32[]{:S(2)}) async-start(), calls=%async_computation.6 | async-start | bytes 2097152 | tf_op jit(solution)/shard_map/psum | solution.py:54
  360.6 60.6 %copy-start.10 = (f32[32768]{0:T(1024)S(1)}, f32[32768]{0:T(1024)}, u32[]{:S(2)}) copy-start(f32[32768]{0:T(1024)} %param.18) | copy-start | bytes 393220
  362.3 111.2 %all-reduce.24.cloned.1.call-start = ((), (), s32[]{:S(2)}) async-start(), calls=%async_computation.7 | async-start | bytes 262144 | tf_op jit(solution)/shard_map/psum | solution.py:70
  421.2 6.5 %copy-start.2 = (f32[8,32768]{1,0:T(8,128)S(1)}, f32[8,32768]{1,0:T(8,128)}, u32[]{:S(2)}) copy-start(f32[8,32768]{1,0:T(8,128)} %all-reduce.22.cloned.1.call-done) | copy-start | bytes 3145732
  429.5 1.9 copy-start.13
  429.5 44.1 %copy-start.6 = (f32[8,4096]{1,0:T(8,128)S(1)}, f32[8,4096]{1,0:T(8,128)}, u32[]{:S(2)}) copy-start(f32[8,4096]{1,0:T(8,128)} %all-reduce.12.cloned.1.call-done) | copy-start | bytes 393220
  429.5 44.1 %copy-start.7 = (f32[8,4096]{1,0:T(8,128)S(1)}, f32[8,4096]{1,0:T(8,128)}, u32[]{:S(2)}) copy-start(f32[8,4096]{1,0:T(8,128)} %all-reduce.16.cloned.1.call-done) | copy-start | bytes 393220
  429.5 44.1 %copy-start.8 = (f32[8,4096]{1,0:T(8,128)S(1)}, f32[8,4096]{1,0:T(8,128)}, u32[]{:S(2)}) copy-start(f32[8,4096]{1,0:T(8,128)} %all-reduce.20.cloned.1.call-done) | copy-start | bytes 393220
  429.5 44.1 %copy-start.9 = (bf16[4,8,4096]{2,1,0:T(8,128)(2,1)S(1)}, bf16[4,8,4096]{2,1,0:T(8,128)(2,1)}, u32[]{:S(2)}) copy-start(bf16[4,8,4096]{2,1,0:T(8,128)(2,1)} %param.21) | copy-start | bytes 786436
Sparse Core Ops, SparseCore 0:
  13.8 61.4 all-reduce.9
  82.3 40.9 all-reduce.11
  129.0 58.8 all-reduce.13
  196.6 40.9 all-reduce.15
  245.4 58.8 all-reduce.17
  313.2 40.9 all-reduce.19
  362.4 58.7 all-reduce.21
  432.5 40.9 all-reduce.23
where the time goes:
time: 527 us; the launch traced here: 526 us
  waiting for transfers between devices  391 us (74%)
  blocking collectives  39.3 us (7%)
  other arithmetic  30.2 us (6%)
  between operations  27.7 us (5%)
  local copies, waits for them, and re-layouts  20.8 us (4%)
  matrix products  16.1 us (3%)
    psum x4, waiting for transfers between devices, per_device(): column_part = lax.psum(summed.reshape(rhs_count, col_tiles * width), 'con')  235 us
    psum x4, waiting for transfers between devices, per_device(): lax.psum(apply_summed.reshape(rhs_count, row_tiles * width), 'var')  156 us
    psum x1, blocking collectives, per_device(): term_pair = lax.psum(term_pair, ('con', 'var'))  39.3 us
    reshape x4, other arithmetic, per_device(): masked.astype(jnp.bfloat16).reshape(rhs_count, col_tiles, width)  12.7 us
  transfers between devices with their start and end apart: 8, of which 8 were waited for; matrix products, arithmetic and copies ran while one was open for 0% of the time, Pallas kernels for 0%

commit v1 on v0

v1 whole, which is shorter than its diff:
```python
import functools
import math

import jax
import jax.numpy as jnp
from jax import lax
from jax.experimental import pallas as pl
from jax.experimental.pallas import tpu as pltpu
from jax.sharding import PartitionSpec as P

MESH = pl.DeviceIdType.MESH
F32 = jnp.float32
BF16 = jnp.bfloat16


def kernel(
    n_con,
    n_var,
    row_s,
    col_s,
    count_s,
    psteps,
    dsteps,
    row_v,
    col_v,
    blocks,
    cost,
    demand,
    x_saved,
    y_saved,
    x_active,
    y_active,
    x_cot,
    y_cot,
    x_out,
    y_out,
    g_out,
    idx,
    onehot,
    row_onehot,
    prod,
    terms,
    row_terms,
    p_tiles,
    u_tiles,
    s_tiles,
    w_tiles,
    partial,
    g_con,
    g_var,
    idx_send,
    idx_recv,
    con_send,
    con_recv,
    var_send,
    var_recv,
    gc_send,
    gc_recv,
    gv_send,
    gv_recv,
):
    slots, width, _ = blocks.shape
    rhs = x_cot.shape[0]
    col_tiles = x_cot.shape[1] // width
    row_tiles = y_cot.shape[1] // width
    steps = y_active.shape[0]
    chips = n_con // 2
    me = lax.axis_index("con")
    mine = lax.axis_index("var")
    core = lax.rem(me, 2)
    chip = lax.div(me, 2)
    sibling = chip * 2 + 1 - core
    scale = 1.0 / math.sqrt(rhs * x_cot.shape[1] * n_var)
    y_weight = scale / n_var
    x_weight = scale / n_con

    def con_peer(offset):
        return lax.rem(me + offset, n_con)

    def var_peer(offset):
        return lax.rem(mine + offset, n_var)

    def chip_peer(offset):
        return lax.rem(chip + offset, chips) * 2 + core

    def con_copy(ref, send, recv, source, target):
        return pltpu.make_async_remote_copy(
            src_ref=ref.at[source],
            dst_ref=ref.at[source],
            send_sem=send,
            recv_sem=recv.at[source],
            device_id={"con": target},
            device_id_type=MESH,
        )

    def var_copy(ref, send, recv, source, target):
        return pltpu.make_async_remote_copy(
            src_ref=ref.at[source],
            dst_ref=ref.at[source],
            send_sem=send,
            recv_sem=recv.at[source],
            device_id={"var": target},
            device_id_type=MESH,
        )

    barrier = pltpu.get_barrier_semaphore()
    for offset in range(1, n_con):
        pl.semaphore_signal(
            barrier, inc=1, device_id={"con": con_peer(offset)}, device_id_type=MESH
        )
    for offset in range(1, n_var):
        pl.semaphore_signal(
            barrier, inc=1, device_id={"var": var_peer(offset)}, device_id_type=MESH
        )

    count = count_s[0, 0]
    slot_lane = lax.broadcasted_iota(jnp.int32, (1, slots), 1)
    own_cols = jnp.where(slot_lane < count, col_v[...], -1)
    own_rows = jnp.where(slot_lane < count, row_v[...], -1)
    idx[me] = jnp.broadcast_to(
        jnp.concatenate([own_cols, own_cols], axis=1), (8, 2 * slots)
    )
    row_onehot[...] = (
        lax.broadcasted_iota(jnp.int32, (row_tiles, 2 * slots), 0)
        == jnp.concatenate([own_rows, own_rows], axis=1)
    ).astype(F32).astype(BF16)

    def first(c, acc):
        cols = pl.ds(pl.multiple_of(c * width, width), width)
        w = y_active[steps - 1, :, cols].astype(F32) * y_cot[:, cols]
        w_tiles[c] = w
        return acc + w * demand[:, cols]

    w_acc = lax.fori_loop(0, row_tiles, first, jnp.zeros((rhs, width), F32))

    pl.semaphore_wait(barrier, n_con - 1 + n_var - 1)
    for offset in range(1, n_con):
        con_copy(idx, idx_send.at[offset - 1], idx_recv, me, con_peer(offset)).start()

    unroll = 8

    def step(i, w_acc):
        k = steps - 1 - i
        terms_k = terms.at[k]
        row_terms_k = row_terms.at[k]
        con_send_k = con_send.at[k]
        con_recv_k = con_recv.at[k]
        var_send_k = var_send.at[k]
        var_recv_k = var_recv.at[k]
        tau_step = psteps[k]
        sigma_step = dsteps[k]

        def down(g, carry):
            for o in range(unroll):
                t = g * unroll + o
                v = w_tiles[row_s[0, t]].astype(BF16)
                prod[pl.ds(t, rhs, stride=slots), :] = jnp.dot(
                    v, blocks[t], preferred_element_type=F32
                )
            return carry

        lax.fori_loop(0, slots // unroll, down, 0)
        terms_k[me] = prod[...].astype(BF16)
        for offset in range(1, chips):
            con_copy(
                terms_k, con_send_k.at[offset - 1], con_recv_k, me, chip_peer(offset)
            ).start()
        con_copy(terms_k, con_send_k.at[chips - 1], con_recv_k, me, sibling).start()

        @pl.when(i == 0)
        def _():
            for offset in range(1, n_con):
                source = con_peer(offset)
                con_copy(idx, idx_send.at[offset - 1], idx_recv, source, source).wait_recv()
            lane = lax.broadcasted_iota(jnp.int32, (1, 2 * slots), 1)
            for pair in range(chips):
                both = jnp.where(
                    lane < slots, idx[2 * pair, 0:1, :], idx[2 * pair + 1, 0:1, :]
                )
                onehot[:, pl.ds(pair * 2 * slots, 2 * slots)] = (
                    lax.broadcasted_iota(jnp.int32, (col_tiles, 2 * slots), 0) == both
                ).astype(F32).astype(BF16)
            for offset in range(1, n_con):
                con_copy(
                    idx, idx_send.at[offset - 1], idx_recv, me, con_peer(offset)
                ).wait_send()

        for offset in range(1, chips):
            source = chip_peer(offset)
            con_copy(
                terms_k, con_send_k.at[chips + offset - 1], con_recv_k, source, sibling
            ).wait_recv()
            con_copy(
                terms_k, con_send_k.at[chips + offset - 1], con_recv_k, source, sibling
            ).start()
        for offset in range(chips):
            source = lax.rem(chip + offset, chips) * 2 + 1 - core
            con_copy(terms_k, con_send_k.at[0], con_recv_k, source, sibling).wait_recv()

        for r in range(rhs):
            right = jnp.concatenate(
                [terms_k[d, pl.ds(r * slots, slots), :] for d in range(n_con)], axis=0
            )
            p_tiles[pl.ds(r, col_tiles, stride=rhs), :] = jnp.dot(
                onehot[...], right, preferred_element_type=F32
            )

        source_x = x_out

        def columns(g, accs):
            ext_acc, cost_acc = accs
            for o in range(unroll):
                c = g * unroll + o
                cols = pl.ds(pl.multiple_of(c * width, width), width)
                rows = pl.ds(pl.multiple_of(c * rhs, rhs), rhs)
                p = p_tiles[rows, :]
                later = x_saved[k + 1, :, cols].astype(F32)
                earlier = x_saved[k, :, cols].astype(F32)
                ext_acc = ext_acc + p * (2.0 * later - earlier)
                q = x_active[k, :, cols].astype(F32) * (
                    source_x[:, cols] - 2.0 * sigma_step * p
                )
                u_tiles[c] = q
                cost_acc = cost_acc + q * cost[:, cols]
                x_out[:, cols] = q + sigma_step * p
            return ext_acc, cost_acc

        zero = jnp.zeros((rhs, width), F32)
        ext_acc, cost_acc = lax.fori_loop(
            0, col_tiles // unroll, columns, (zero, zero)
        )

        def across(g, carry):
            for o in range(unroll):
                t = g * unroll + o
                u = u_tiles[col_s[0, t]].astype(BF16)
                prod[pl.ds(t, rhs, stride=slots), :] = lax.dot_general(
                    u, blocks[t], (((1,), (1,)), ((), ())), preferred_element_type=F32
                )
            return carry

        lax.fori_loop(0, slots // unroll, across, 0)
        for r in range(rhs):
            slab = prod[pl.ds(r * slots, slots), :]
            high = slab.astype(BF16)
            low = (slab - high.astype(F32)).astype(BF16)
            s_tiles[pl.ds(r, row_tiles, stride=rhs), :] = jnp.dot(
                row_onehot[...],
                jnp.concatenate([high, low], axis=0),
                preferred_element_type=F32,
            )
        row_terms_k[mine] = s_tiles[...].astype(BF16)
        for offset in range(1, n_var):
            var_copy(
                row_terms_k, var_send_k.at[offset - 1], var_recv_k, mine, var_peer(offset)
            ).start()

        def dual_dot(c, acc):
            cols = pl.ds(pl.multiple_of(c * width, width), width)
            rows = pl.ds(pl.multiple_of(c * rhs, rhs), rhs)
            return acc + s_tiles[rows, :] * y_saved[k, :, cols].astype(F32)

        s_acc = lax.fori_loop(0, row_tiles, dual_dot, zero)
        partial[pl.ds(k, 1), :] = jnp.sum(
            scale * s_acc - x_weight * cost_acc, axis=0, keepdims=True
        )
        partial[pl.ds(steps + k, 1), :] = jnp.sum(
            y_weight * w_acc - x_weight * ext_acc, axis=0, keepdims=True
        )

        for offset in range(1, n_var):
            source = var_peer(offset)
            var_copy(
                row_terms_k, var_send_k.at[offset - 1], var_recv_k, source, source
            ).wait_recv()
        total = row_terms_k[0].astype(F32)
        for j in range(1, n_var):
            total = total + row_terms_k[j].astype(F32)
        s_tiles[...] = total
        before = jnp.maximum(k - 1, 0)

        def rows_loop(c, acc):
            cols = pl.ds(pl.multiple_of(c * width, width), width)
            rows = pl.ds(pl.multiple_of(c * rhs, rhs), rhs)
            y_bar = w_tiles[c] + tau_step * s_tiles[rows, :]
            y_out[:, cols] = y_bar
            w = y_active[before, :, cols].astype(F32) * y_bar
            w_tiles[c] = w
            return acc + w * demand[:, cols]

        w_acc = lax.fori_loop(0, row_tiles, rows_loop, zero)

        for offset in range(2 * chips - 1):
            con_copy(terms_k, con_send_k.at[offset], con_recv_k, me, sibling).wait_send()
        for offset in range(1, n_var):
            var_copy(
                row_terms_k, var_send_k.at[offset - 1], var_recv_k, mine, var_peer(offset)
            ).wait_send()
        return w_acc

    x_out[...] = x_cot[...]
    lax.fori_loop(0, steps, step, w_acc)

    g_con[me] = partial[...]
    for offset in range(1, n_con):
        con_copy(g_con, gc_send.at[offset - 1], gc_recv, me, con_peer(offset)).start()
    for offset in range(1, n_con):
        source = con_peer(offset)
        con_copy(g_con, gc_send.at[offset - 1], gc_recv, source, source).wait_recv()
    sums = g_con[0]
    for d in range(1, n_con):
        sums = sums + g_con[d]
    g_var[mine] = sums
    for offset in range(1, n_var):
        var_copy(g_var, gv_send.at[offset - 1], gv_recv, mine, var_peer(offset)).start()
    for offset in range(1, n_var):
        source = var_peer(offset)
        var_copy(g_var, gv_send.at[offset - 1], gv_recv, source, source).wait_recv()
    sums = g_var[0]
    for j in range(1, n_var):
        sums = sums + g_var[j]
    for n in range(2 * steps):
        g_out[n // steps, n % steps] = jnp.sum(sums[n : n + 1, :])
    for offset in range(1, n_con):
        con_copy(g_con, gc_send.at[offset - 1], gc_recv, me, con_peer(offset)).wait_send()
    for offset in range(1, n_var):
        var_copy(g_var, gv_send.at[offset - 1], gv_recv, mine, var_peer(offset)).wait_send()


def per_device(
    tile_values,
    tile_row,
    tile_col,
    tile_count,
    unit_cost,
    demand,
    x_saved,
    y_saved,
    x_active,
    y_active,
    x_cot,
    y_cot,
    primal_step,
    dual_step,
):
    blocks = tile_values.reshape(tile_values.shape[2:])
    slots, width, _ = blocks.shape
    rhs = x_cot.shape[0]
    col_tiles = x_cot.shape[1] // width
    row_tiles = y_cot.shape[1] // width
    steps = primal_step.shape[0]
    n_con = lax.axis_size("con")
    n_var = lax.axis_size("var")
    chips = n_con // 2
    rows = tile_row.reshape(1, slots)
    cols = tile_col.reshape(1, slots)
    vmem = pl.BlockSpec(memory_space=pltpu.VMEM)
    smem = pl.BlockSpec(memory_space=pltpu.SMEM)
    dma = pltpu.SemaphoreType.DMA
    return pl.pallas_call(
        functools.partial(kernel, n_con, n_var),
        out_shape=(
            jax.ShapeDtypeStruct(x_cot.shape, F32),
            jax.ShapeDtypeStruct(y_cot.shape, F32),
            jax.ShapeDtypeStruct((2, steps), F32),
        ),
        in_specs=[smem] * 5 + [vmem] * 11,
        out_specs=(vmem, vmem, smem),
        scratch_shapes=[
            pltpu.VMEM((n_con, 8, 2 * slots), jnp.int32),
            pltpu.VMEM((col_tiles, n_con * slots), BF16),
            pltpu.VMEM((row_tiles, 2 * slots), BF16),
            pltpu.VMEM((rhs * slots, width), F32),
            pltpu.VMEM((steps, n_con, rhs * slots, width), BF16),
            pltpu.VMEM((steps, n_var, rhs * row_tiles, width), BF16),
            pltpu.VMEM((rhs * col_tiles, width), F32),
            pltpu.VMEM((col_tiles, rhs, width), F32),
            pltpu.VMEM((rhs * row_tiles, width), F32),
            pltpu.VMEM((row_tiles, rhs, width), F32),
            pltpu.VMEM((2 * steps, width), F32),
            pltpu.VMEM((n_con, 2 * steps, width), F32),
            pltpu.VMEM((n_var, 2 * steps, width), F32),
            dma((n_con - 1,)),
            dma((n_con,)),
            dma((steps, 2 * chips - 1)),
            dma((steps, n_con)),
            dma((steps, n_var - 1)),
            dma((steps, n_var)),
            dma((n_con - 1,)),
            dma((n_con,)),
            dma((n_var - 1,)),
            dma((n_var,)),
        ],
        compiler_params=pltpu.CompilerParams(
            collective_id=0, has_side_effects=True, vmem_limit_bytes=56 * 1024 * 1024
        ),
    )(
        rows,
        cols,
        tile_count.reshape(1, 1),
        primal_step,
        dual_step,
        rows,
        cols,
        blocks,
        unit_cost.reshape(1, unit_cost.shape[0]),
        demand,
        x_saved,
        y_saved,
        x_active,
        y_active,
        x_cot,
        y_cot,
    )


def solution(mesh):
    in_specs = (
        P("con", "var", "groups", None, None),
        P("con", "var", "groups"),
        P("con", "var", "groups"),
        P("con", "var", "groups"),
        P(("groups", "var")),
        P("groups", "con"),
        P(None, "groups", "var"),
        P(None, "groups", "con"),
        P(None, "groups", "var"),
        P(None, "groups", "con"),
        P("groups", "var"),
        P("groups", "con"),
        P(),
        P(),
    )
    out_specs = (P("groups", "var"), P("groups", "con"), P("groups", None))
    return jax.shard_map(
        per_device, mesh=mesh, in_specs=in_specs, out_specs=out_specs, check_vma=False
    )
```

time: 527 us -> 127 us (0.24)
  waiting for transfers between devices: 391 us -> 0 us
  Pallas kernels: 0 us -> 120 us
  blocking collectives: 39.3 us -> 0 us
  other arithmetic: 30.2 us -> 0 us
  between operations: 27.7 us -> 1.29 us
  matrix products: 16.1 us -> 0 us
  local copies, waits for them, and re-layouts: 20.8 us -> 5.05 us
    psum x8 -> x0, waiting for transfers between devices: 391 us -> none  [the longest x4 235 us: per_device(): column_part = lax.psum(summed.reshape(rhs_count, col_tiles * width), 'con')]
    pallas_call x0 -> x1, Pallas kernels: none -> 120 us  [per_device(): pl.pallas_call(functools.partial(kernel, n_con, n_var), out_shape=(jax.Sh...]
    psum x1 -> x0, blocking collectives: 39.3 us -> none  [per_device(): term_pair = lax.psum(term_pair, ('con', 'var'))]
    reshape x8 -> x0, other arithmetic: 17.5 us -> none  [the longest x4 12.7 us: per_device(): masked.astype(jnp.bfloat16).reshape(rhs_count, col_tiles, width)]
    dot_general x16 -> x0, matrix products: 16.1 us -> none  [the longest x4 4.73 us: per_device(): jnp.einsum('tab,rtb->rta', blocks, apply_pieces, preferred_element_type=j...]
    reduce_sum x3 -> x0, other arithmetic: 11.9 us -> none  [the longest x1 6.48 us: per_device(): jnp.sum(column_part * extrapolated)]
    gather x8 -> x0, local copies, waits for them, and re-layouts: 9.52 us -> none  [the longest x4 5.72 us: per_device(): masked.astype(jnp.bfloat16).reshape(rhs_count, col_tiles, width)]
  transfers between devices with their start and end apart: 8 -> 0, of which waited for: 8 -> 0; matrix products, arithmetic and copies ran while one was open for 0% -> 0% of each run, Pallas kernels for 0% -> 0%
where the time goes in v1:
time: 127 us
  Pallas kernels  120 us (94%)
  local copies, waits for them, and re-layouts  5.05 us (4%)
  between operations  1.29 us (1%)
    pallas_call x1, Pallas kernels, per_device(): pl.pallas_call(functools.partial(kernel, n_con, n_var), out_shape=(jax.Sh...  120 us
    unnamed x3, local copies, waits for them, and re-layouts  5.05 us

profile of v1, /device:TPU:0, one launch (start us, length us, event | category | flops | bytes accessed | tf_op | source)
XLA Modules:
  0.0 126.7 jit_solution(4708243274003036735)
XLA Ops:
  1.3 120.3 %shard_map.157 = (f32[8,32768]{1,0:T(8,128)}, f32[8,4096]{1,0:T(8,128)}, f32[2,4]{1,0:T(2,128)}) custom-call(s32[1,64]{1,0:T(1,128)} %bitcast.8, s32[1,64]{1,0:T(1,128)} %bitcast.10, s32[1,1]{1,0:T(1,128)} %bitcast.5.count_s, f32[4]{0:T(128)} %psteps.1, f32[4]{0:T(128)} %dsteps.1, s32[1,64]{1,0:T(1,128)} %bitcast.9, s32[1,64]{1,0:T(1,128)} %bitcast.11, ...), custom_call_target="tpu_custom_call" | custom-call | tf_op jit(solution)/shard_map/pallas_call | solution.py:360
  121.6 2.3 %copy.21 = f32[8,32768]{1,0:T(8,128)} copy(f32[8,32768]{1,0:T(8,128)} %get-tuple-element.6) | data formatting | bytes 2097152
  123.9 1.6 %copy.22 = f32[8,4096]{1,0:T(8,128)} copy(f32[8,4096]{1,0:T(8,128)} %get-tuple-element.7) | data formatting | bytes 262144
  125.5 1.2 copy.23

commit v2 on v1

--- a/solution.py
+++ b/solution.py
@@ -11,6 +11,7 @@
 MESH = pl.DeviceIdType.MESH
 F32 = jnp.float32
 BF16 = jnp.bfloat16
+PIECES = 4
 
 
 def kernel(
@@ -23,18 +24,27 @@
     dsteps,
     row_v,
     col_v,
+    blocks_hbm,
+    cost_hbm,
+    demand,
+    x_saved_hbm,
+    y_saved,
+    x_active_hbm,
+    y_active,
+    x_cot_hbm,
+    y_cot,
+    x_hbm,
+    y_out,
+    g_out,
     blocks,
     cost,
-    demand,
     x_saved,
-    y_saved,
     x_active,
-    y_active,
-    x_cot,
-    y_cot,
     x_out,
-    y_out,
-    g_out,
+    load_sem,
+    saved_sem,
+    active_sem,
+    store_sem,
     idx,
     onehot,
     row_onehot,
@@ -60,28 +70,47 @@
     gv_recv,
 ):
     slots, width, _ = blocks.shape
-    rhs = x_cot.shape[0]
-    col_tiles = x_cot.shape[1] // width
+    rhs = x_out.shape[0]
+    col_tiles = x_out.shape[1] // width
     row_tiles = y_cot.shape[1] // width
     steps = y_active.shape[0]
     chips = n_con // 2
+    piece = rhs * slots // PIECES
     me = lax.axis_index("con")
     mine = lax.axis_index("var")
     core = lax.rem(me, 2)
     chip = lax.div(me, 2)
     sibling = chip * 2 + 1 - core
-    scale = 1.0 / math.sqrt(rhs * x_cot.shape[1] * n_var)
+    scale = 1.0 / math.sqrt(rhs * x_out.shape[1] * n_var)
     y_weight = scale / n_var
     x_weight = scale / n_con
 
+    def load(source, target, sem):
+        return pltpu.make_async_copy(source, target, sem)
+
+    def load_saved(k):
+        return load(x_saved_hbm.at[k], x_saved.at[k], saved_sem.at[k])
+
+    def load_active(k):
+        return load(x_active_hbm.at[k], x_active.at[k], active_sem.at[k])
+
+    load_blocks = load(blocks_hbm, blocks, load_sem.at[0])
+    load_cot = load(x_cot_hbm, x_out, load_sem.at[1])
+    load_cost = load(cost_hbm, cost, load_sem.at[2])
+    store_x = load(x_out, x_hbm, store_sem.at[0])
+    load_blocks.start()
+    load_saved(steps).start()
+    load_cot.start()
+    load_cost.start()
+    for k in reversed(range(steps)):
+        load_saved(k).start()
+        load_active(k).start()
+
     def con_peer(offset):
         return lax.rem(me + offset, n_con)
 
     def var_peer(offset):
         return lax.rem(mine + offset, n_var)
-
-    def chip_peer(offset):
-        return lax.rem(chip + offset, chips) * 2 + core
 
     def con_copy(ref, send, recv, source, target):
         return pltpu.make_async_remote_copy(
@@ -102,6 +131,30 @@
             device_id={"var": target},
             device_id_type=MESH,
         )
+
+    def chain_copy(k, source, part, way):
+        target = (me + 2, me - 2, sibling)[way]
+        span = pl.ds(part * piece, piece)
+        owner = source * 2 + core
+        return pltpu.make_async_remote_copy(
+            src_ref=terms.at[k, owner, span],
+            dst_ref=terms.at[k, owner, span],
+            send_sem=con_send.at[k, source, part, way],
+            recv_sem=con_recv.at[k, owner, part],
+            device_id={"con": target},
+            device_id_type=MESH,
+        )
+
+    def arrived(k, owner, part):
+        span = pl.ds(part * piece, piece)
+        pltpu.make_async_remote_copy(
+            src_ref=terms.at[k, owner, span],
+            dst_ref=terms.at[k, owner, span],
+            send_sem=con_send.at[k, 0, part, 0],
+            recv_sem=con_recv.at[k, owner, part],
+            device_id={"con": sibling},
+            device_id_type=MESH,
+        ).wait_recv()
 
     barrier = pltpu.get_barrier_semaphore()
     for offset in range(1, n_con):
@@ -143,8 +196,6 @@
         k = steps - 1 - i
         terms_k = terms.at[k]
         row_terms_k = row_terms.at[k]
-        con_send_k = con_send.at[k]
-        con_recv_k = con_recv.at[k]
         var_send_k = var_send.at[k]
         var_recv_k = var_recv.at[k]
         tau_step = psteps[k]
@@ -161,11 +212,18 @@
 
         lax.fori_loop(0, slots // unroll, down, 0)
         terms_k[me] = prod[...].astype(BF16)
-        for offset in range(1, chips):
-            con_copy(
-                terms_k, con_send_k.at[offset - 1], con_recv_k, me, chip_peer(offset)
-            ).start()
-        con_copy(terms_k, con_send_k.at[chips - 1], con_recv_k, me, sibling).start()
+        for part in range(PIECES):
+
+            @pl.when(chip < chips - 1)
+            def _():
+                chain_copy(k, chip, part, 0).start()
+
+            @pl.when(chip > 0)
+            def _():
+                chain_copy(k, chip, part, 1).start()
+
+        for part in range(PIECES):
+            chain_copy(k, chip, part, 2).start()
 
         @pl.when(i == 0)
         def _():
@@ -185,17 +243,41 @@
                     idx, idx_send.at[offset - 1], idx_recv, me, con_peer(offset)
                 ).wait_send()
 
-        for offset in range(1, chips):
-            source = chip_peer(offset)
-            con_copy(
-                terms_k, con_send_k.at[chips + offset - 1], con_recv_k, source, sibling
-            ).wait_recv()
-            con_copy(
-                terms_k, con_send_k.at[chips + offset - 1], con_recv_k, source, sibling
-            ).start()
-        for offset in range(chips):
-            source = lax.rem(chip + offset, chips) * 2 + 1 - core
-            con_copy(terms_k, con_send_k.at[0], con_recv_k, source, sibling).wait_recv()
+        for hop in range(1, chips):
+            for part in range(PIECES):
+
+                @pl.when(chip >= hop)
+                def _():
+                    arrived(k, me - 2 * hop, part)
+
+                    @pl.when(chip < chips - 1)
+                    def _():
+                        chain_copy(k, chip - hop, part, 0).start()
+
+                    chain_copy(k, chip - hop, part, 2).start()
+
+                @pl.when(chip + hop < chips)
+                def _():
+                    arrived(k, me + 2 * hop, part)
+
+                    @pl.when(chip > 0)
+                    def _():
+                        chain_copy(k, chip + hop, part, 1).start()
+
+                    chain_copy(k, chip + hop, part, 2).start()
+
+        for source in range(chips):
+            for part in range(PIECES):
+                arrived(k, source * 2 + 1 - core, part)
+
+        @pl.when(i == 0)
+        def _():
+            load_saved(steps).wait()
+            load_cot.wait()
+            load_cost.wait()
+
+        load_saved(k).wait()
+        load_active(k).wait()
 
         for r in range(rhs):
             right = jnp.concatenate(
@@ -204,8 +286,6 @@
             p_tiles[pl.ds(r, col_tiles, stride=rhs), :] = jnp.dot(
                 onehot[...], right, preferred_element_type=F32
             )
-
-        source_x = x_out
 
         def columns(g, accs):
             ext_acc, cost_acc = accs
@@ -218,7 +298,7 @@
                 earlier = x_saved[k, :, cols].astype(F32)
                 ext_acc = ext_acc + p * (2.0 * later - earlier)
                 q = x_active[k, :, cols].astype(F32) * (
-                    source_x[:, cols] - 2.0 * sigma_step * p
+                    x_out[:, cols] - 2.0 * sigma_step * p
                 )
                 u_tiles[c] = q
                 cost_acc = cost_acc + q * cost[:, cols]
@@ -229,6 +309,10 @@
         ext_acc, cost_acc = lax.fori_loop(
             0, col_tiles // unroll, columns, (zero, zero)
         )
+
+        @pl.when(k == 0)
+        def _():
+            store_x.start()
 
         def across(g, carry):
             for o in range(unroll):
@@ -268,6 +352,14 @@
             y_weight * w_acc - x_weight * ext_acc, axis=0, keepdims=True
         )
 
+        @pl.when(k == 0)
+        def _():
+            g_con[me] = partial[...]
+            for offset in range(1, n_con):
+                con_copy(
+                    g_con, gc_send.at[offset - 1], gc_recv, me, con_peer(offset)
+                ).start()
+
         for offset in range(1, n_var):
             source = var_peer(offset)
             var_copy(
@@ -290,20 +382,28 @@
 
         w_acc = lax.fori_loop(0, row_tiles, rows_loop, zero)
 
-        for offset in range(2 * chips - 1):
-            con_copy(terms_k, con_send_k.at[offset], con_recv_k, me, sibling).wait_send()
+        for source in range(chips):
+            for part in range(PIECES):
+
+                @pl.when(jnp.logical_and(source <= chip, chip < chips - 1))
+                def _():
+                    chain_copy(k, source, part, 0).wait_send()
+
+                @pl.when(jnp.logical_and(source >= chip, chip > 0))
+                def _():
+                    chain_copy(k, source, part, 1).wait_send()
+
+                chain_copy(k, source, part, 2).wait_send()
+
         for offset in range(1, n_var):
             var_copy(
                 row_terms_k, var_send_k.at[offset - 1], var_recv_k, mine, var_peer(offset)
             ).wait_send()
         return w_acc
 
-    x_out[...] = x_cot[...]
+    load_blocks.wait()
     lax.fori_loop(0, steps, step, w_acc)
 
-    g_con[me] = partial[...]
-    for offset in range(1, n_con):
-        con_copy(g_con, gc_send.at[offset - 1], gc_recv, me, con_peer(offset)).start()
     for offset in range(1, n_con):
         source = con_peer(offset)
         con_copy(g_con, gc_send.at[offset - 1], gc_recv, source, source).wait_recv()
@@ -325,6 +425,7 @@
         con_copy(g_con, gc_send.at[offset - 1], gc_recv, me, con_peer(offset)).wait_send()
     for offset in range(1, n_var):
         var_copy(g_var, gv_send.at[offset - 1], gv_recv, mine, var_peer(offset)).wait_send()
+    store_x.wait()
 
 
 def per_device(
@@ -356,6 +457,7 @@
     cols = tile_col.reshape(1, slots)
     vmem = pl.BlockSpec(memory_space=pltpu.VMEM)
     smem = pl.BlockSpec(memory_space=pltpu.SMEM)
+    hbm = pl.BlockSpec(memory_space=pl.ANY)
     dma = pltpu.SemaphoreType.DMA
     return pl.pallas_call(
         functools.partial(kernel, n_con, n_var),
@@ -364,9 +466,19 @@
             jax.ShapeDtypeStruct(y_cot.shape, F32),
             jax.ShapeDtypeStruct((2, steps), F32),
         ),
-        in_specs=[smem] * 5 + [vmem] * 11,
-        out_specs=(vmem, vmem, smem),
+        in_specs=[smem] * 5
+        + [vmem, vmem, hbm, hbm, vmem, hbm, vmem, hbm, vmem, hbm, vmem],
+        out_specs=(hbm, vmem, smem),
         scratch_shapes=[
+            pltpu.VMEM((slots, width, width), BF16),
+            pltpu.VMEM((1, x_cot.shape[1]), F32),
+            pltpu.VMEM(x_saved.shape, BF16),
+            pltpu.VMEM(x_active.shape, jnp.int32),
+            pltpu.VMEM(x_cot.shape, F32),
+            dma((3,)),
+            dma((steps + 1,)),
+            dma((steps,)),
+            dma((1,)),
             pltpu.VMEM((n_con, 8, 2 * slots), jnp.int32),
             pltpu.VMEM((col_tiles, n_con * slots), BF16),
             pltpu.VMEM((row_tiles, 2 * slots), BF16),
@@ -382,8 +494,8 @@
             pltpu.VMEM((n_var, 2 * steps, width), F32),
             dma((n_con - 1,)),
             dma((n_con,)),
-            dma((steps, 2 * chips - 1)),
-            dma((steps, n_con)),
+            dma((steps, chips, PIECES, 3)),
+            dma((steps, n_con, PIECES)),
             dma((steps, n_var - 1)),
             dma((steps, n_var)),
             dma((n_con - 1,)),

time: 127 us -> 111 us (0.87)
  Pallas kernels: 120 us -> 104 us
    pallas_call x1, Pallas kernels: 120 us -> 104 us  [per_device(): pl.pallas_call(functools.partial(kernel, n_con, n_var), out_shape=(jax.Sh...]
where the time goes in v2:
time: 111 us
  Pallas kernels  104 us (94%)
  local copies, waits for them, and re-layouts  5.05 us (5%)
  between operations  1.29 us (1%)
    pallas_call x1, Pallas kernels, per_device(): pl.pallas_call(functools.partial(kernel, n_con, n_var), out_shape=(jax.Sh...  104 us
    unnamed x3, local copies, waits for them, and re-layouts  5.05 us

profile of v2, /device:TPU:0, one launch (start us, length us, event | category | flops | bytes accessed | tf_op | source)
XLA Modules:
  0.0 110.6 jit_solution(17998454111400437071)
XLA Ops:
  1.3 104.3 %shard_map.157 = (f32[8,32768]{1,0:T(8,128)}, f32[8,4096]{1,0:T(8,128)}, f32[2,4]{1,0:T(2,128)}) custom-call(s32[1,64]{1,0:T(1,128)} %bitcast.8, s32[1,64]{1,0:T(1,128)} %bitcast.10, s32[1,1]{1,0:T(1,128)} %bitcast.5.count_s, f32[4]{0:T(128)} %psteps.1, f32[4]{0:T(128)} %dsteps.1, s32[1,64]{1,0:T(1,128)} %bitcast.9, s32[1,64]{1,0:T(1,128)} %bitcast.11, ...), custom_call_target="tpu_custom_call" | custom-call | tf_op jit(solution)/shard_map/pallas_call | solution.py:462
  105.5 2.3 %copy.21 = f32[8,32768]{1,0:T(8,128)} copy(f32[8,32768]{1,0:T(8,128)} %get-tuple-element.6) | data formatting | bytes 2097152
  107.8 1.6 %copy.22 = f32[8,4096]{1,0:T(8,128)} copy(f32[8,4096]{1,0:T(8,128)} %get-tuple-element.7) | data formatting | bytes 262144
  109.4 1.2 %copy.23 = f32[2,4]{1,0:T(2,128)} copy(f32[2,4]{1,0:T(2,128)} %get-tuple-element.8) | data formatting | bytes 64

commit v3 on v2

--- a/solution.py
+++ b/solution.py
@@ -184,13 +184,31 @@
         w_tiles[c] = w
         return acc + w * demand[:, cols]
 
-    w_acc = lax.fori_loop(0, row_tiles, first, jnp.zeros((rhs, width), F32))
+    w_acc = lax.fori_loop(0, row_tiles, first, jnp.zeros((rhs, width), F32), unroll=8)
 
     pl.semaphore_wait(barrier, n_con - 1 + n_var - 1)
     for offset in range(1, n_con):
         con_copy(idx, idx_send.at[offset - 1], idx_recv, me, con_peer(offset)).start()
 
     unroll = 8
+    group = slots // PIECES
+    zeros = jnp.zeros((rhs, width), F32)
+
+    def diagonal(one, two):
+        return jnp.concatenate(
+            [
+                jnp.concatenate([one, zeros], axis=1),
+                jnp.concatenate([zeros, two], axis=1),
+            ],
+            axis=0,
+        ).astype(BF16)
+
+    def pair_row(t, part):
+        return part * piece + t - part * group
+
+    def keep(row, both):
+        prod[pl.ds(row, rhs, stride=group), :] = both[:rhs]
+        prod[pl.ds(row + 1, rhs, stride=group), :] = both[rhs:]
 
     def step(i, w_acc):
         k = steps - 1 - i
@@ -201,18 +219,18 @@
         tau_step = psteps[k]
         sigma_step = dsteps[k]
 
-        def down(g, carry):
-            for o in range(unroll):
-                t = g * unroll + o
-                v = w_tiles[row_s[0, t]].astype(BF16)
-                prod[pl.ds(t, rhs, stride=slots), :] = jnp.dot(
-                    v, blocks[t], preferred_element_type=F32
+        for part in range(PIECES):
+            for pair in range(part * group // 2, (part + 1) * group // 2):
+                t = 2 * pair
+                left = diagonal(w_tiles[row_s[0, t]], w_tiles[row_s[0, t + 1]])
+                both = jnp.dot(
+                    left,
+                    blocks[pl.ds(t, 2)].reshape(2 * width, width),
+                    preferred_element_type=F32,
                 )
-            return carry
-
-        lax.fori_loop(0, slots // unroll, down, 0)
-        terms_k[me] = prod[...].astype(BF16)
-        for part in range(PIECES):
+                keep(pair_row(t, part), both)
+            span = pl.ds(part * piece, piece)
+            terms_k[me, span] = prod[span, :].astype(BF16)
 
             @pl.when(chip < chips - 1)
             def _():
@@ -279,53 +297,63 @@
         load_saved(k).wait()
         load_active(k).wait()
 
-        for r in range(rhs):
-            right = jnp.concatenate(
-                [terms_k[d, pl.ds(r * slots, slots), :] for d in range(n_con)], axis=0
+        def stacked(r):
+            return jnp.concatenate(
+                [
+                    terms_k[d, pl.ds(part * piece + r * group, group), :]
+                    for d in range(n_con)
+                    for part in range(PIECES)
+                ],
+                axis=0,
             )
-            p_tiles[pl.ds(r, col_tiles, stride=rhs), :] = jnp.dot(
-                onehot[...], right, preferred_element_type=F32
+
+        for r in range(0, rhs, 2):
+            spread = jnp.dot(
+                onehot[...],
+                jnp.concatenate([stacked(r), stacked(r + 1)], axis=1),
+                preferred_element_type=F32,
             )
-
-        def columns(g, accs):
-            ext_acc, cost_acc = accs
+            p_tiles[pl.ds(r, col_tiles, stride=rhs), :] = spread[:, :width]
+            p_tiles[pl.ds(r + 1, col_tiles, stride=rhs), :] = spread[:, width:]
+
+        def columns(g, carry):
             for o in range(unroll):
                 c = g * unroll + o
                 cols = pl.ds(pl.multiple_of(c * width, width), width)
                 rows = pl.ds(pl.multiple_of(c * rhs, rhs), rhs)
                 p = p_tiles[rows, :]
-                later = x_saved[k + 1, :, cols].astype(F32)
-                earlier = x_saved[k, :, cols].astype(F32)
-                ext_acc = ext_acc + p * (2.0 * later - earlier)
                 q = x_active[k, :, cols].astype(F32) * (
                     x_out[:, cols] - 2.0 * sigma_step * p
                 )
                 u_tiles[c] = q
-                cost_acc = cost_acc + q * cost[:, cols]
                 x_out[:, cols] = q + sigma_step * p
-            return ext_acc, cost_acc
-
-        zero = jnp.zeros((rhs, width), F32)
-        ext_acc, cost_acc = lax.fori_loop(
-            0, col_tiles // unroll, columns, (zero, zero)
-        )
+            return carry
+
+        lax.fori_loop(0, col_tiles // unroll, columns, 0)
 
         @pl.when(k == 0)
         def _():
             store_x.start()
 
-        def across(g, carry):
-            for o in range(unroll):
-                t = g * unroll + o
-                u = u_tiles[col_s[0, t]].astype(BF16)
-                prod[pl.ds(t, rhs, stride=slots), :] = lax.dot_general(
-                    u, blocks[t], (((1,), (1,)), ((), ())), preferred_element_type=F32
+        for part in range(PIECES):
+            for pair in range(part * group // 2, (part + 1) * group // 2):
+                t = 2 * pair
+                left = diagonal(u_tiles[col_s[0, t]], u_tiles[col_s[0, t + 1]])
+                both = lax.dot_general(
+                    left,
+                    jnp.concatenate([blocks[t], blocks[t + 1]], axis=1),
+                    (((1,), (1,)), ((), ())),
+                    preferred_element_type=F32,
                 )
-            return carry
-
-        lax.fori_loop(0, slots // unroll, across, 0)
+                keep(pair_row(t, part), both)
         for r in range(rhs):
-            slab = prod[pl.ds(r * slots, slots), :]
+            slab = jnp.concatenate(
+                [
+                    prod[pl.ds(part * piece + r * group, group), :]
+                    for part in range(PIECES)
+                ],
+                axis=0,
+            )
             high = slab.astype(BF16)
             low = (slab - high.astype(F32)).astype(BF16)
             s_tiles[pl.ds(r, row_tiles, stride=rhs), :] = jnp.dot(
@@ -344,7 +372,22 @@
             rows = pl.ds(pl.multiple_of(c * rhs, rhs), rhs)
             return acc + s_tiles[rows, :] * y_saved[k, :, cols].astype(F32)
 
-        s_acc = lax.fori_loop(0, row_tiles, dual_dot, zero)
+        def column_dots(g, accs):
+            ext_acc, cost_acc = accs
+            for o in range(unroll):
+                c = g * unroll + o
+                cols = pl.ds(pl.multiple_of(c * width, width), width)
+                rows = pl.ds(pl.multiple_of(c * rhs, rhs), rhs)
+                later = x_saved[k + 1, :, cols].astype(F32)
+                earlier = x_saved[k, :, cols].astype(F32)
+                ext_acc = ext_acc + p_tiles[rows, :] * (2.0 * later - earlier)
+                cost_acc = cost_acc + u_tiles[c] * cost[:, cols]
+            return ext_acc, cost_acc
+
+        s_acc = lax.fori_loop(0, row_tiles, dual_dot, zeros, unroll=4)
+        ext_acc, cost_acc = lax.fori_loop(
+            0, col_tiles // unroll, column_dots, (zeros, zeros)
+        )
         partial[pl.ds(k, 1), :] = jnp.sum(
             scale * s_acc - x_weight * cost_acc, axis=0, keepdims=True
         )
@@ -380,7 +423,7 @@
             w_tiles[c] = w
             return acc + w * demand[:, cols]
 
-        w_acc = lax.fori_loop(0, row_tiles, rows_loop, zero)
+        w_acc = lax.fori_loop(0, row_tiles, rows_loop, zeros, unroll=8)
 
         for source in range(chips):
             for part in range(PIECES):

time: 111 us -> 98.5 us (0.89)
  Pallas kernels: 104 us -> 92 us
    pallas_call x1, Pallas kernels: 104 us -> 92 us  [per_device(): pl.pallas_call(functools.partial(kernel, n_con, n_var), out_shape=(jax.Sh...]
where the time goes in v3:
time: 98.5 us; the launch traced here: 98.3 us
  Pallas kernels  92 us (93%)
  local copies, waits for them, and re-layouts  5.05 us (5%)
  between operations  1.29 us (1%)
    pallas_call x1, Pallas kernels, per_device(): pl.pallas_call(functools.partial(kernel, n_con, n_var), out_shape=(jax.Sh...  92 us
    unnamed x3, local copies, waits for them, and re-layouts  5.05 us

profile of v3, /device:TPU:0, one launch (start us, length us, event | category | flops | bytes accessed | tf_op | source)
XLA Modules:
  0.0 98.3 jit_solution(4782934315595100654)
XLA Ops:
  1.3 92.0 %shard_map.157 = (f32[8,32768]{1,0:T(8,128)}, f32[8,4096]{1,0:T(8,128)}, f32[2,4]{1,0:T(2,128)}) custom-call(s32[1,64]{1,0:T(1,128)} %bitcast.8, s32[1,64]{1,0:T(1,128)} %bitcast.10, s32[1,1]{1,0:T(1,128)} %bitcast.5.count_s, f32[4]{0:T(128)} %psteps.1, f32[4]{0:T(128)} %dsteps.1, s32[1,64]{1,0:T(1,128)} %bitcast.9, s32[1,64]{1,0:T(1,128)} %bitcast.11, ...), custom_call_target="tpu_custom_call" | custom-call | tf_op jit(solution)/shard_map/pallas_call | solution.py:505
  93.3 2.3 %copy.21 = f32[8,32768]{1,0:T(8,128)} copy(f32[8,32768]{1,0:T(8,128)} %get-tuple-element.6) | data formatting | bytes 2097152
  95.5 1.6 %copy.22 = f32[8,4096]{1,0:T(8,128)} copy(f32[8,4096]{1,0:T(8,128)} %get-tuple-element.7) | data formatting | bytes 262144
  97.1 1.2 %copy.23 = f32[2,4]{1,0:T(2,128)} copy(f32[2,4]{1,0:T(2,128)} %get-tuple-element.8) | data formatting | bytes 64
